TPU v7x, 128 devices: a whole 4x4x4 slice. The times are simulated.
128 devices in a mesh: lat: 8 (over z, x_lo), lon: 16 (over x_hi, y, core).
Axes of the slice: x: 4 (x_hi: 2, x_lo: 2; x = x_hi * 2 + x_lo), y: 4, z: 4, core: 2. Of those that a mesh axis runs over, the one named last changes fastest.
Arguments:
- latent: bfloat16 [4, 48, 384, 512], P(None, 'lat', 'lon'), may hold values from -40 to 40
- cotangent: bfloat16 [4, 48, 384, 512], P(None, 'lat', 'lon'), may hold values from -6 to 6
- qkv_weight: bfloat16 [512, 1536], replicated, may hold values from -0.25 to 0.25
- out_weight: bfloat16 [512, 512], replicated, may hold values from -0.25 to 0.25
- up_weight: bfloat16 [512, 2048], replicated, may hold values from -0.25 to 0.25
- down_weight: bfloat16 [2048, 512], replicated, may hold values from -0.125 to 0.125
- earth_bias: float32 [8, 2, 8, 20736], P('lat'), may hold values from -8 to 400
Outputs:
- out: bfloat16 [4, 48, 384, 512], P(None, 'lat', 'lon')
- grad_latent: bfloat16 [4, 48, 384, 512], P(None, 'lat', 'lon')
- weight_grad: float32 [3145728], P(('lat', 'lon'))
- bias_grad: float32 [8, 2, 8, 20736], P('lat')
All inputs are finite; a program needn't handle non-finite values.
Results may differ from a plain program's by a relative error of at most 0.024.
Values may be sent and summed in bfloat16 or wider, within the bound.
No kernel may reach another device: no remote copies, remote signals or barrier semaphores. Data moves between devices by JAX's collectives and lax.ppermute only.
A program may use at most 128 MiB of HBM per device.

v0:
```python
import math

import jax
import jax.numpy as jnp
from jax import lax
from jax.sharding import PartitionSpec as P

WIN_LEV = 2
WIN_LAT = 6
WIN_LON = 12


norm_eps = 1e-05
masked_score = -1000000000.0


def from_behind(x, axis, by):
    peers = lax.axis_size(axis)
    return lax.ppermute(x, axis, [(i, (i + by) % peers) for i in range(peers)])


def batched(form, left, right):
    return jnp.einsum(form, left, right, preferred_element_type=jnp.float32)


def matmul(left, right):
    return jnp.dot(left, right, preferred_element_type=jnp.float32)


def normalize(values):
    center = values - jnp.mean(values, axis=-1, keepdims=True)
    inv_std = lax.rsqrt(jnp.mean(center * center, axis=-1, keepdims=True) + norm_eps)
    return (center * inv_std, inv_std)


def norm_back(normed, inv_std, upstream):
    mean_grad = jnp.mean(upstream, axis=-1, keepdims=True)
    mean_prod = jnp.mean(upstream * normed, axis=-1, keepdims=True)
    return inv_std * (upstream - mean_grad - normed * mean_prod)


def gelu_exact(values):
    return values * 0.5 * (1.0 + jax.scipy.special.erf(values * 0.7071067811865476))


def gelu_slope(values):
    cumulative = 0.5 * (1.0 + jax.scipy.special.erf(values * 0.7071067811865476))
    density = jnp.exp(-0.5 * values * values) * 0.3989422804014327
    return cumulative + values * density


def to_windows(field, win_lev, win_lat, win_lon):
    levels, rows, cols = field.shape[:3]
    tail = field.shape[3:]
    shaped = field.reshape(
        (levels // win_lev, win_lev, rows // win_lat, win_lat, cols // win_lon, win_lon) + tail
    )
    order = (2, 0, 4, 1, 3, 5) + tuple(range(6, 6 + len(tail)))
    moved = shaped.transpose(order)
    return moved.reshape(
        (rows // win_lat, levels // win_lev, cols // win_lon, win_lev * win_lat * win_lon) + tail
    )


def from_windows(windows, levels, rows, cols, win_lev, win_lat, win_lon):
    tail = windows.shape[4:]
    shaped = windows.reshape(
        (rows // win_lat, levels // win_lev, cols // win_lon, win_lev, win_lat, win_lon) + tail
    )
    order = (1, 3, 0, 4, 2, 5) + tuple(range(6, 6 + len(tail)))
    return shaped.transpose(order).reshape((levels, rows, cols) + tail)


def group_codes(levels, rows, cols, row_start, total_rows, lev_shift, lat_shift):
    level_pos = lax.broadcasted_iota(jnp.int32, (levels, rows, cols), 0)
    row_pos = lax.broadcasted_iota(jnp.int32, (levels, rows, cols), 1) + row_start
    wrap_level = (level_pos >= levels - lev_shift).astype(jnp.int32)
    wrap_row = (row_pos >= total_rows - lat_shift).astype(jnp.int32)
    return 2 * wrap_level + wrap_row


def window_pass(
    tokens,
    upstream,
    codes,
    bias_rows,
    qkv_weight,
    out_weight,
    up_weight,
    down_weight,
    win_lev,
    win_lat,
    win_lon,
):
    levels, rows, cols, width = tokens.shape
    heads = bias_rows.shape[2]
    head_dim = width // heads
    win_tok = win_lev * win_lat * win_lon
    lat_wins = rows // win_lat
    lev_wins = levels // win_lev
    lon_wins = cols // win_lon
    groups = lat_wins * lev_wins * lon_wins
    count = groups * win_tok
    tok_win = to_windows(tokens, win_lev, win_lat, win_lon).reshape(count, width)
    grad_win = to_windows(upstream, win_lev, win_lat, win_lon).reshape(count, width)
    code_win = to_windows(codes, win_lev, win_lat, win_lon).reshape(groups, win_tok)
    bias_all = jnp.broadcast_to(
        bias_rows[:, :, None], (lat_wins, lev_wins, lon_wins, heads, win_tok * win_tok)
    )
    bias_all = bias_all.reshape(groups, heads, win_tok, win_tok)
    scale = head_dim ** (-0.5)
    tok_float = tok_win.astype(jnp.float32)
    normed_one, inv_one = normalize(tok_float)
    normed_low = normed_one.astype(jnp.bfloat16)
    projected = matmul(normed_low, qkv_weight).astype(jnp.bfloat16)
    query = projected[:, :width].reshape(groups, win_tok, heads, head_dim)
    keys = projected[:, width : 2 * width].reshape(groups, win_tok, heads, head_dim)
    values = projected[:, 2 * width :].reshape(groups, win_tok, heads, head_dim)
    scores = batched("gqhc,gkhc->ghqk", query, keys) * scale + bias_all
    allowed = code_win[:, None, :, None] == code_win[:, None, None, :]
    scores = jnp.where(allowed, scores, masked_score)
    peak = jnp.max(scores, axis=-1, keepdims=True)
    expo = jnp.exp(scores - peak)
    probs = expo / jnp.sum(expo, axis=-1, keepdims=True)
    probs_low = probs.astype(jnp.bfloat16)
    mixed = batched("ghqk,gkhc->gqhc", probs_low, values).reshape(count, width).astype(jnp.bfloat16)
    resid = tok_float + matmul(mixed, out_weight)
    normed_two, inv_two = normalize(resid)
    normed_low_two = normed_two.astype(jnp.bfloat16)
    hidden_pre = matmul(normed_low_two, up_weight)
    hidden_low = gelu_exact(hidden_pre).astype(jnp.bfloat16)
    result = (resid + matmul(hidden_low, down_weight)).astype(jnp.bfloat16)
    grad_float = grad_win.astype(jnp.float32)
    grad_down = matmul(hidden_low.T, grad_win)
    grad_hidden = (matmul(grad_win, down_weight.T) * gelu_slope(hidden_pre)).astype(jnp.bfloat16)
    grad_up = matmul(normed_low_two.T, grad_hidden)
    grad_resid = grad_float + norm_back(normed_two, inv_two, matmul(grad_hidden, up_weight.T))
    grad_resid_low = grad_resid.astype(jnp.bfloat16)
    grad_out = matmul(mixed.T, grad_resid_low)
    grad_mixed = (
        matmul(grad_resid_low, out_weight.T)
        .astype(jnp.bfloat16)
        .reshape(groups, win_tok, heads, head_dim)
    )
    grad_probs = batched("gqhc,gkhc->ghqk", grad_mixed, values)
    grad_values = batched("ghqk,gqhc->gkhc", probs_low, grad_mixed)
    grad_scores = probs * (grad_probs - jnp.sum(grad_probs * probs, axis=-1, keepdims=True))
    grad_scaled = (grad_scores * scale).astype(jnp.bfloat16)
    grad_query = batched("ghqk,gkhc->gqhc", grad_scaled, keys)
    grad_keys = batched("ghqk,gqhc->gkhc", grad_scaled, query)
    grad_proj = jnp.concatenate(
        [
            grad_query.reshape(count, width),
            grad_keys.reshape(count, width),
            grad_values.reshape(count, width),
        ],
        axis=1,
    ).astype(jnp.bfloat16)
    grad_qkv = matmul(normed_low.T, grad_proj)
    grad_tokens = (
        grad_resid + norm_back(normed_one, inv_one, matmul(grad_proj, qkv_weight.T))
    ).astype(jnp.bfloat16)
    grad_bias = jnp.sum(
        grad_scores.reshape(lat_wins, lev_wins, lon_wins, heads, win_tok * win_tok), axis=2
    )
    result_field = from_windows(
        result.reshape(lat_wins, lev_wins, lon_wins, win_tok, width),
        levels,
        rows,
        cols,
        win_lev,
        win_lat,
        win_lon,
    )
    grad_field = from_windows(
        grad_tokens.reshape(lat_wins, lev_wins, lon_wins, win_tok, width),
        levels,
        rows,
        cols,
        win_lev,
        win_lat,
        win_lon,
    )
    return (result_field, grad_field, grad_bias, (grad_qkv, grad_out, grad_up, grad_down))


def rows_ahead(stack):
    half = WIN_LAT // 2
    arrived = from_behind(stack[:, :, :half], "lat", -1)
    return jnp.concatenate([stack[:, :, half:], arrived], axis=2)


def cols_ahead(stack):
    half = WIN_LON // 2
    arrived = from_behind(stack[:, :, :, :half], "lon", -1)
    return jnp.concatenate([stack[:, :, :, half:], arrived], axis=3)


def rows_back(stack):
    half = WIN_LAT // 2
    arrived = from_behind(stack[:, :, -half:], "lat", 1)
    return jnp.concatenate([arrived, stack[:, :, :-half]], axis=2)


def cols_back(stack):
    half = WIN_LON // 2
    arrived = from_behind(stack[:, :, :, -half:], "lon", 1)
    return jnp.concatenate([arrived, stack[:, :, :, :-half]], axis=3)


def advance(stack):
    stack = jnp.roll(stack, -(WIN_LEV // 2), axis=1)
    return cols_ahead(rows_ahead(stack))


def retreat(stack):
    stack = cols_back(rows_back(stack))
    return jnp.roll(stack, WIN_LEV // 2, axis=1)


def body(latent, cotangent, qkv_weight, out_weight, up_weight, down_weight, earth_bias):
    levels, rows, cols, width = latent.shape
    moved = advance(jnp.stack([latent, cotangent]))
    row_start = lax.axis_index("lat") * rows
    total_rows = rows * lax.axis_size("lat")
    codes = group_codes(levels, rows, cols, row_start, total_rows, WIN_LEV // 2, WIN_LAT // 2)
    result, grad_tok, grad_bias, grads = window_pass(
        moved[0],
        moved[1],
        codes,
        earth_bias,
        qkv_weight,
        out_weight,
        up_weight,
        down_weight,
        WIN_LEV,
        WIN_LAT,
        WIN_LON,
    )
    returned = retreat(jnp.stack([result, grad_tok]))
    all_tokens = levels * total_rows * cols * lax.axis_size("lon")
    flat = jnp.concatenate([piece.reshape(-1) for piece in grads]) * (1.0 / math.sqrt(all_tokens))
    weight_grad = lax.psum_scatter(flat, ("lat", "lon"), scatter_dimension=0, tiled=True)
    bias_grad = lax.psum(grad_bias.astype(jnp.bfloat16), "lon").astype(jnp.float32)
    return (returned[0], returned[1], weight_grad, bias_grad)


def solution(mesh):
    in_specs = (
        P(None, "lat", "lon", None),
        P(None, "lat", "lon", None),
        P(),
        P(),
        P(),
        P(),
        P("lat", None, None, None),
    )
    out_specs = (
        P(None, "lat", "lon", None),
        P(None, "lat", "lon", None),
        P(("lat", "lon")),
        P("lat", None, None, None),
    )
    return jax.shard_map(body, mesh=mesh, in_specs=in_specs, out_specs=out_specs, check_vma=False)
```

profile of v0, /device:TPU:1, one launch (start us, length us, event | category | flops | bytes accessed | tf_op | source)
XLA Modules:
  0.0 497.0 jit_solution(4679293791041035280)
XLA Ops:
  9.9 5.5 %collective-permute-start = (bf16[2,4,3,24,512]{4,3,2,1,0:T(8,128)(2,1)}, bf16[2,4,3,24,512]{4,3,2,1,0:T(8,128)(2,1)S(1)}, u32[]{:S(2)}, u32[]{:S(2)}) collective-permute-start(bf16[2,4,3,24,512]{4,3,2,1,0:T(8,128)(2,1)} %get-tuple-element.26), channel_id=1, source_target_pairs={{0,112},{16,0},{32,16},{48,32},{64,48},{80,64},{96,80},{112,96},{1... | collective-permute-start | bytes 1769480 | tf_op jit(solution)/shard_map/ppermute | solution.py:19
  15.5 3.0 broadcast_in_dim.20
  18.6 6.2 %broadcast_in_dim.21 = f32[4,8,144,144]{3,2,1,0:T(8,128)} reshape(f32[2,2,8,20736]{3,2,1,0:T(8,128)} %broadcast_in_dim.20) | data formatting | bytes 5308416 | tf_op jit(solution)/shard_map/broadcast_in_dim | solution.py:107
  24.7 6.2 %copy.65 = f32[4,8,144,144]{2,3,1,0:T(8,128)} copy(f32[4,8,144,144]{3,2,1,0:T(8,128)} %broadcast_in_dim.21) | data formatting | bytes 5308416 | tf_op jit(solution)/shard_map/broadcast_in_dim | solution.py:107
  32.6 6.2 %collective-permute-done.1 = bf16[2,4,6,6,512]{4,3,2,1,0:T(8,128)(2,1)S(1)} collective-permute-done((bf16[2,4,6,6,512]{4,3,2,1,0:T(8,128)(2,1)S(1)}, bf16[2,4,6,6,512]{4,3,2,1,0:T(8,128)(2,1)S(1)}, u32[]{:S(2)}, u32[]{:S(2)}) %collective-permute-start.1) | collective-permute-done | bytes 294944 | tf_op jit(solution)/shard_map/ppermute | solution.py:19
  40.3 2.7 reshape.163
  44.2 2.4 multiply_reduce_fusion.4
  47.9 2.6 reshape_squeeze.4
  50.5 2.1 copy.71
  52.5 2.0 reshape_reshape.11
  57.6 3.0 convolution_convert_fusion
  61.9 2.5 reshape.166
  66.2 2.8 reshape.165
  69.0 2.6 copy.63
  71.5 2.5 reshape.164
  74.0 2.7 copy.66
  76.8 3.6 add_select_fusion
  80.5 3.0 fusion.39
  84.0 6.0 %fusion.7 = bf16[4,144,8,64]{1,3,2,0:T(8,128)(2,1)} fusion(bf16[4,144,8,64]{1,3,2,0:T(8,128)(2,1)S(1)} %copy-done.19, f32[4,8,144]{2,1,0:T(8,128)S(1)} %get-tuple-element.27, f32[4,8,144,144]{2,3,1,0:T(8,128)} %copy-done.3), kind=kOutput, calls=%fused_computation.26 | convolution fusion | flops 87224976 | bytes 3852288 | tf_op jit(solution)/shard_map/ghqk,gkhc->gqhc/dot_general | solution.py:23
  90.0 2.0 copy.68
  93.6 2.2 fusion.40
  96.2 3.3 multiply_convert_fusion.1
  99.5 3.1 fusion.6
  107.4 3.9 convolution_bitcast_fusion.1
  113.0 2.9 copy.73
  115.9 6.4 %fusion.10 = bf16[4,144,8,64]{1,3,2,0:T(8,128)(2,1)} fusion(bf16[4,144,8,64]{1,3,2,0:T(8,128)(2,1)} %copy.73, f32[4,8,144]{2,1,0:T(8,128)S(1)} %get-tuple-element.27, f32[4,8,144,144]{2,3,1,0:T(8,128)} %copy-done.3), kind=kOutput, calls=%fused_computation.29 | convolution fusion | flops 87224976 | bytes 3852288 | tf_op jit(solution)/shard_map/ghqk,gqhc->gkhc/dot_general | solution.py:23
  122.3 4.1 multiply_reduce_fusion
  131.8 6.2 %copy.85 = f32[4,8,144,144]{3,2,1,0:T(8,128)} copy(f32[4,8,144,144]{2,3,1,0:T(8,128)} %copy-done.2) | data formatting | bytes 5308416 | tf_op jit(solution)/shard_map/mul | solution.py:147
  137.9 2.6 copy.100
  142.3 2.3 reshape.155
  144.6 5.2 %copy.101 = f32[64,16,8,128]{3,1,2,0:T(8,128)} copy(f32[64,16,8,128]{3,2,1,0:T(8,128)} %convolution_bitcast_fusion.1) | data formatting | bytes 8388608
  151.7 3.0 copy.102
  156.5 3.2 reshape.154
  159.7 6.6 %reshape.160 = f32[2,2,8,20736]{3,2,1,0:T(8,128)} reshape(f32[4,8,144,144]{3,2,1,0:T(8,128)} %copy.85) | data formatting | bytes 5308416 | tf_op jit(solution)/shard_map/reshape | solution.py:164
  166.3 3.0 copy.77
  169.3 3.0 reshape.153
  172.3 3.0 reduce_sum.109
  179.2 3.3 fusion.28
  182.6 4.6 reshape.156
  187.1 12.0 %maximum_multiply_fusion = f32[3145728]{0:T(1024)} fusion(f32[1048576]{0:T(1024)} %bitcast.89, f32[1048576]{0:T(1024)} %bitcast.88, f32[262144]{0:T(1024)} %bitcast.91, f32[786432]{0:T(1024)} %reshape.156), kind=kLoop, calls=%fused_computation.1 | loop fusion | flops 12582912 | bytes 25165824 | tf_op jit(solution)/shard_map/mul | solution.py:242
  199.2 4.5 fusion.11
  206.4 2.8 stack_reshape.6
  209.2 3.6 fusion.34
  215.2 14.6 %collective-permute-done.2 = bf16[2,4,3,24,512]{4,1,3,2,0:T(4,128)(2,1)S(1)} collective-permute-done((bf16[2,4,3,24,512]{4,1,3,2,0:T(4,128)(2,1)S(1)}, bf16[2,4,3,24,512]{4,1,3,2,0:T(4,128)(2,1)S(1)}, u32[]{:S(2)}, u32[]{:S(2)}) %collective-permute-start.2) | collective-permute-done | bytes 589856 | tf_op jit(solution)/shard_map/ppermute | solution.py:19
  230.0 2.9 collective-permute-start.3
  233.0 80.3 %all-reduce.4.cloned.1.call-done = bf16[1,2,8,20736]{3,2,1,0:T(8,128)(2,1)} async-done(((bf16[1,2,8,20736]{3,2,1,0:T(8,128)(2,1)}), bf16[1,2,8,20736]{3,2,1,0:T(8,128)(2,1)}) %all-reduce.4.cloned.1.call-update) | async-done | bytes 663568 | tf_op jit(solution)/shard_map/psum | solution.py:244
  313.3 2.2 convert_element_type.110
  320.1 168.2 %all-reduce.6.cloned.1.call-done = f32[3145728]{0:T(1024)} async-done(((f32[3145728]{0:T(1024)}), f32[3145728]{0:T(1024)}) %all-reduce.6.cloned.1.call-update) | async-done | bytes 12582928
  (121 shorter events, 49.4 us)
Async XLA Ops:
  7.2 89.0 %copy-start = (bf16[512,2048]{1,0:T(8,128)(2,1)S(1)}, bf16[512,2048]{1,0:T(8,128)(2,1)}, u32[]{:S(2)}) copy-start(bf16[512,2048]{1,0:T(8,128)(2,1)} %param.11) | copy-start | bytes 6291460
  7.2 1.5 copy-start.13
  7.2 1.6 copy-start.14
  7.2 306.1 %all-reduce.4.cloned.1.call-start = ((), (), s32[]{:S(2)}) async-start(), calls=%async_computation | async-start | bytes 1327104 | tf_op jit(solution)/shard_map/psum | solution.py:244
  9.9 21.1 %collective-permute-start = (bf16[2,4,3,24,512]{4,3,2,1,0:T(8,128)(2,1)}, bf16[2,4,3,24,512]{4,3,2,1,0:T(8,128)(2,1)S(1)}, u32[]{:S(2)}, u32[]{:S(2)}) collective-permute-start(bf16[2,4,3,24,512]{4,3,2,1,0:T(8,128)(2,1)} %get-tuple-element.26), channel_id=1, source_target_pairs={{0,112},{16,0},{32,16},{48,32},{64,48},{80,64},{96,80},{112,96},{1... | collective-permute-start | bytes 1769480 | tf_op jit(solution)/shard_map/ppermute | solution.py:19
  30.9 7.8 %collective-permute-start.1 = (bf16[2,4,6,6,512]{4,3,2,1,0:T(8,128)(2,1)S(1)}, bf16[2,4,6,6,512]{4,3,2,1,0:T(8,128)(2,1)S(1)}, u32[]{:S(2)}, u32[]{:S(2)}) collective-permute-start(bf16[2,4,6,6,512]{4,3,2,1,0:T(8,128)(2,1)S(1)} %pad_maximum_fusion.4), channel_id=1, source_target_pairs={{0,15},{1,0},{2,1},{3,2},{4,3},{5,4},{6,5},{7,6},{8,7},{9,8},{10,9... | collective-permute-start | bytes 884744 | tf_op jit(solution)/shard_map/ppermute | solution.py:19
  43.0 3.6 copy-start.12
  57.6 3.0 copy-start.4
  66.2 10.6 %copy-start.7 = (bf16[4,144,8,64]{1,3,2,0:T(8,128)(2,1)}, bf16[4,144,8,64]{1,3,2,0:T(8,128)(2,1)S(1)}, u32[]{:S(2)}) copy-start(bf16[4,144,8,64]{1,3,2,0:T(8,128)(2,1)S(1)} %copy.64) | copy-start | bytes 1769476
  80.4 3.6 copy-start.3
  80.4 3.6 copy-start.19
  96.2 3.3 copy-start.16
  96.2 3.3 copy-start.22
  104.3 1.1 copy-start.10
  105.4 1.6 copy-start.18
  122.3 4.2 slice-start
  122.3 4.3 slice-start.1
  126.6 1.2 copy-start.9
  127.8 2.5 copy-start.2
  127.8 2.5 copy-start.8
  137.9 2.6 copy-start.20
  144.6 5.2 %copy-start.17 = (bf16[576,512]{1,0:T(8,128)(2,1)S(1)}, bf16[576,512]{1,0:T(8,128)(2,1)}, u32[]{:S(2)}) copy-start(bf16[576,512]{1,0:T(8,128)(2,1)} %reshape_reshape.11) | copy-start | bytes 1769476
  144.6 5.2 %copy-start.23 = (bf16[576,2048]{1,0:T(8,128)(2,1)S(1)}, bf16[576,2048]{1,0:T(8,128)(2,1)}, u32[]{:S(2)}) copy-start(bf16[576,2048]{1,0:T(8,128)(2,1)} %get-tuple-element.31) | copy-start | bytes 7077892
  151.7 3.0 copy-start.11
  175.3 313.0 %all-reduce.6.cloned.1.call-start = ((), (), s32[]{:S(2)}) async-start(), calls=%async_computation.1 | async-start | bytes 25165824
  175.4 3.8 copy-start.5
  177.9 1.3 copy-start.21
  203.7 5.5 %copy-start.6 = (f32[576,512]{1,0:T(8,128)S(1)}, f32[576,512]{1,0:T(8,128)}, u32[]{:S(2)}) copy-start(f32[576,512]{1,0:T(8,128)} %copy-done.4) | copy-start | bytes 3538948
  213.2 1.1 copy-start.15
  215.1 14.7 %collective-permute-start.2 = (bf16[2,4,3,24,512]{4,1,3,2,0:T(4,128)(2,1)S(1)}, bf16[2,4,3,24,512]{4,1,3,2,0:T(4,128)(2,1)S(1)}, u32[]{:S(2)}, u32[]{:S(2)}) collective-permute-start(bf16[2,4,3,24,512]{4,1,3,2,0:T(4,128)(2,1)S(1)} %get-tuple-element.23), channel_id=1, source_target_pairs={{0,16},{16,32},{32,48},{48,64},{64,80},{80,96},{96,112},{112,0},{1... | collective-permute-start | bytes 1769480 | tf_op jit(solution)/shard_map/ppermute | solution.py:19
  230.0 85.5 %collective-permute-start.3 = (bf16[2,4,6,6,512]{4,1,3,2,0:T(4,128)(2,1)S(1)}, bf16[2,4,6,6,512]{4,1,3,2,0:T(4,128)(2,1)S(1)}, u32[]{:S(2)}, u32[]{:S(2)}) collective-permute-start(bf16[2,4,6,6,512]{4,1,3,2,0:T(4,128)(2,1)S(1)} %pad_maximum_fusion.5), channel_id=1, source_target_pairs={{0,1},{1,2},{2,3},{3,4},{4,5},{5,6},{6,7},{7,8},{8,9},{9,10},{10,1... | collective-permute-start | bytes 884744 | tf_op jit(solution)/shard_map/ppermute | solution.py:19
  317.0 172.9 %copy-start.1 = (bf16[512,2048]{1,0:T(8,128)(2,1)S(1)}, bf16[512,2048]{1,0:T(8,128)(2,1)}, u32[]{:S(2)}) copy-start(bf16[512,2048]{1,0:T(8,128)(2,1)} %param.11) | copy-start | bytes 6291460
Sparse Core Ops, SparseCore 0:
  175.5 137.7 all-reduce.3
  318.9 169.3 all-reduce.5
where the time goes:
time: 501 us; the launch traced here: 497 us
  waiting for transfers between devices  269 us (54%)
  local copies, waits for them, and re-layouts  115 us (23%)
  matrix products  56 us (11%)
  other arithmetic  31.9 us (6%)
  between operations  14.8 us (3%)
  starting transfers between devices  9.8 us (2%)
    unnamed x3, waiting for transfers between devices  168 us
    psum x1, waiting for transfers between devices, body(): lax.psum(grad_bias.astype(jnp.bfloat16), 'lon').astype(jnp.float32)  80.3 us
    dot_general x12, matrix products, matmul(): return jnp.dot(left, right, preferred_element_type=jnp.float32)  32.5 us
    dot_general x6, matrix products, batched(): return jnp.einsum(form, left, right, preferred_element_type=jnp.float32)  23.4 us
    ppermute x4, waiting for transfers between devices, from_behind(): return lax.ppermute(x, axis, [(i, (i + by) % peers) for i in range(peers)])  20.8 us
    unnamed x61, local copies, waits for them, and re-layouts  20.5 us
    broadcast_in_dim x3, local copies, waits for them, and re-layouts, window_pass(): jnp.broadcast_to(bias_rows[:, :, None], (lat_wins, lev_wins, lon_wins, he...  15.4 us
    mul x1, other arithmetic, body(): jnp.concatenate([piece.reshape(-1) for piece in grads])  12 us
  transfers between devices with their start and end apart: 6, of which 4 were waited for; matrix products, arithmetic and copies ran while one was open for 12% of the time, Pallas kernels for 0%

commit v1 on v0

v1 whole, which is shorter than its diff:
```python
import functools
import math

import jax
import jax.numpy as jnp
import ml_dtypes
import numpy as np
from jax import lax
from jax.experimental import pallas as pl
from jax.experimental.pallas import tpu as pltpu
from jax.sharding import PartitionSpec as P

WIDTH = 512
HIDDEN = 2048
HEADS = 8
LEVELS = 4
ROWS = 6
COLS = 24
WIN_LEV = 2
WIN_LAT = 6
WIN_LON = 12
WTOK = 144
TOKENS = LEVELS * ROWS * COLS
HALF_LAT = WIN_LAT // 2
HALF_LON = WIN_LON // 2
EDGE = 8
BAND = LEVELS * HALF_LAT * COLS
SIDE = LEVELS * HALF_LAT * EDGE
GROUP = 4
GWIDTH = GROUP * WIDTH // HEADS
GTOK = GROUP * WTOK
WINDOWS = 4
CHUNK = 48
norm_eps = 1e-05
masked_score = -1000000000.0
f32 = jnp.float32
bf16 = jnp.bfloat16


def dot(left, right):
    return lax.dot_general(left, right, (((1,), (0,)), ((), ())), preferred_element_type=f32)


def dot_nt(left, right):
    return lax.dot_general(left, right, (((1,), (1,)), ((), ())), preferred_element_type=f32)


def dot_tn(left, right):
    return lax.dot_general(left, right, (((0,), (0,)), ((), ())), preferred_element_type=f32)


def normalize(values):
    center = values - jnp.mean(values, axis=-1, keepdims=True)
    inv_std = lax.rsqrt(jnp.mean(center * center, axis=-1, keepdims=True) + norm_eps)
    return (center * inv_std, inv_std)


def norm_back(normed, inv_std, upstream):
    mean_grad = jnp.mean(upstream, axis=-1, keepdims=True)
    mean_prod = jnp.mean(upstream * normed, axis=-1, keepdims=True)
    return inv_std * (upstream - mean_grad - normed * mean_prod)


def token_tables():
    pick = np.zeros((TOKENS, TOKENS + BAND + 2 * SIDE), np.float32)
    spread = np.zeros((2 * BAND + 2 * SIDE, TOKENS), np.float32)
    for lev in range(LEVELS):
        src_lev = (lev + 1) % LEVELS
        for i in range(ROWS):
            for j in range(COLS):
                b, lv = divmod(lev, WIN_LEV)
                c, jj = divmod(j, WIN_LON)
                w = (b * 2 + c) * WTOK + (lv * WIN_LAT + i) * WIN_LON + jj
                inner_row = i < HALF_LAT
                inner_col = j < COLS - HALF_LON
                band_row = src_lev * HALF_LAT + (i if inner_row else i - HALF_LAT)
                wide = band_row * COLS + j + HALF_LON
                narrow = band_row * EDGE + j - (COLS - HALF_LON)
                if inner_row and inner_col:
                    pick[w, (src_lev * ROWS + i + HALF_LAT) * COLS + j + HALF_LON] = 1
                    spread[wide, w] = 1
                elif inner_col:
                    pick[w, TOKENS + wide] = 1
                    spread[BAND + wide, w] = 1
                elif inner_row:
                    pick[w, TOKENS + BAND + narrow] = 1
                    spread[2 * BAND + narrow, w] = 1
                else:
                    pick[w, TOKENS + BAND + SIDE + narrow] = 1
                    spread[2 * BAND + SIDE + narrow, w] = 1
    return pick.astype(ml_dtypes.bfloat16), spread.astype(ml_dtypes.bfloat16)


def loop(count, step):
    lax.fori_loop(0, count, lambda i, carry: (step(i), carry)[1], 0)


def at(index, size):
    return pl.ds(pl.multiple_of(index * size, size), size)


def gather_tokens(pick_ref, cat, own_ref, row_ref, col_ref, cor_ref):
    cat[0:TOKENS, :] = own_ref[...]
    cat[TOKENS : TOKENS + BAND, :] = row_ref[...]
    cat[TOKENS + BAND : TOKENS + BAND + SIDE, :] = col_ref[...]
    cat[TOKENS + BAND + SIDE :, :] = cor_ref[...]
    return dot(pick_ref[...], cat[...])


def head_stack(block):
    lane = lax.broadcasted_iota(jnp.int32, block.shape, 1) // (WIDTH // HEADS)
    zero = jnp.zeros_like(block)
    return jnp.concatenate([jnp.where(lane == h, block, zero) for h in range(GROUP)], axis=0)


def head_join(stacked):
    lane = lax.broadcasted_iota(jnp.int32, (WTOK, GWIDTH), 1) // (WIDTH // HEADS)
    total = stacked[0:WTOK]
    for h in range(1, GROUP):
        total = jnp.where(lane == h, stacked[h * WTOK : (h + 1) * WTOK], total)
    return total


def attend_kernel(
    pick_ref, own_ref, row_ref, col_ref, cor_ref, bias_ref, qkv_ref,
    tok_ref, proj_ref, probs_ref, mixed_ref, cat, normed, scores,
):
    scale = (WIDTH // HEADS) ** (-0.5)
    tok_ref[...] = gather_tokens(pick_ref, cat, own_ref, row_ref, col_ref, cor_ref).astype(bf16)

    def norm_rows(i):
        values, _ = normalize(tok_ref[at(i, 48), :].astype(f32))
        normed[at(i, 48), :] = values.astype(bf16)

    loop(TOKENS // 48, norm_rows)

    def project(i):
        proj_ref[:, at(i, 256)] = dot(normed[...], qkv_ref[:, at(i, 256)]).astype(bf16)

    loop(3 * WIDTH // 256, project)

    def attend(i):
        win, group = i // 2, i % 2
        rows = at(win, WTOK)
        query = head_stack(proj_ref[rows, at(group, GWIDTH)])
        scores[...] = dot_nt(query, proj_ref[rows, at(group + 2, GWIDTH)])
        for h in range(GROUP):
            part = scores[h * WTOK : (h + 1) * WTOK, :] * scale + bias_ref[(win // 2) * HEADS + group * GROUP + h]
            expo = jnp.exp(part - jnp.max(part, axis=-1, keepdims=True))
            part = expo * (1.0 / jnp.sum(expo, axis=-1, keepdims=True))
            probs_ref[i, h * WTOK : (h + 1) * WTOK, :] = part.astype(bf16)
        mixed = dot(probs_ref[i], proj_ref[rows, at(group + 4, GWIDTH)])
        mixed_ref[rows, at(group, GWIDTH)] = head_join(mixed).astype(bf16)

    loop(2 * WINDOWS, attend)


def chunk_id(dy, dx, z, place_ref, other):
    core = place_ref[0]
    core = 1 - core if other else core
    y = lax.rem(place_ref[1] + dy, 4)
    x = lax.rem(place_ref[2] + dx, 4)
    return z * 32 + lax.rem(x, 2) * 16 + (x // 2) * 8 + y * 2 + core


def put_lanes(ref, rows, value):
    for t in range(4):
        ref[t, rows, :] = value[:, t * 128 : (t + 1) * 128]


def mlp_kernel(
    place_ref, pick_ref, spread_ref, own_ref, row_ref, col_ref, cor_ref, tok_ref, mixed_ref,
    out_ref, up_ref, down_ref,
    pieces_ref, gresid_ref, keep_ref, send_ref,
    cat, grad, resid, normed, low, inv, pre, slope, hidden, ghidden, result, wgrad,
):
    grad[...] = gather_tokens(pick_ref, cat, own_ref, row_ref, col_ref, cor_ref).astype(bf16)
    resid[...] = dot(mixed_ref[...], out_ref[...])

    def norm_rows(i):
        rows = at(i, 48)
        total = tok_ref[rows, :].astype(f32) + resid[rows, :]
        resid[rows, :] = total
        values, inv_std = normalize(total)
        normed[rows, :] = values
        inv[rows, :] = jnp.broadcast_to(inv_std, (48, 128))
        low[rows, :] = values.astype(bf16)

    loop(TOKENS // 48, norm_rows)

    def feed(j):
        cols = at(j, WIDTH)
        pre[...] = dot(low[...], up_ref[:, cols])
        slope[...] = dot_nt(grad[...], down_ref[cols, :])

        def gelu(i):
            rows = at(i, 32)
            values = pre[rows, :]
            cumulative = 0.5 * (1.0 + lax.erf(values * 0.7071067811865476))
            hidden[rows, cols] = (values * cumulative).astype(bf16)
            density = jnp.exp(-0.5 * values * values) * 0.3989422804014327
            ghidden[rows, cols] = (slope[rows, :] * (cumulative + values * density)).astype(bf16)

        loop(TOKENS // 32, gelu)
        put_lanes(wgrad, at(j + 5, WIDTH), dot_tn(hidden[:, cols], grad[...]))
        put_lanes(wgrad, pl.ds(WIDTH + j, WIDTH, stride=4), dot_tn(low[...], ghidden[:, cols]))

    for j in range(HIDDEN // WIDTH):
        feed(j)

    def finish(n):
        cols = at(n, 256)
        result[:, cols] = (resid[:, cols] + dot(hidden[...], down_ref[:, cols])).astype(bf16)
        resid[:, cols] = dot_nt(ghidden[...], up_ref[cols, :])

    loop(WIDTH // 256, finish)

    def norm_rows_back(i):
        rows = at(i, 48)
        back = norm_back(normed[rows, :], inv[rows, 0:1], resid[rows, :])
        total = grad[rows, :].astype(f32) + back
        gresid_ref[rows, :] = total
        low[rows, :] = total.astype(bf16)

    loop(TOKENS // 48, norm_rows_back)
    pieces_ref[...] = dot(spread_ref[...], result[...]).astype(bf16)
    put_lanes(wgrad, slice(0, WIDTH), dot_tn(mixed_ref[...], low[...]))

    def share(i):
        dy, dx, z = i // 12, lax.rem(i // 3, 4), lax.rem(i, 3)
        for other, ref in ((False, keep_ref), (True, send_ref)):
            chunk = at(chunk_id(dy, dx, z, place_ref, other), CHUNK)
            for t in range(4):
                ref[at(i, CHUNK), t * 128 : (t + 1) * 128] = wgrad[t, chunk, :].astype(bf16)

    loop(48, share)


def attend_back_kernel(
    place_ref, proj_ref, probs_ref, gresid_ref, out_ref,
    gproj_ref, keep_ref, send_ref, gmixed, gprobs, gscores, bias,
):
    scale = (WIDTH // HEADS) ** (-0.5)
    gmixed[...] = dot_nt(gresid_ref[...].astype(bf16), out_ref[...]).astype(bf16)

    def back(i):
        lev, group = i // 2, lax.rem(i, 2)
        for c in range(2):
            win = lev * 2 + c
            rows = at(win, WTOK)
            probs = win * 2 + group
            upstream = head_stack(gmixed[rows, at(group, GWIDTH)])
            gprobs[...] = dot_nt(upstream, proj_ref[rows, at(group + 4, GWIDTH)])
            for h in range(GROUP):
                part = slice(h * WTOK, (h + 1) * WTOK)
                prob = probs_ref[probs, part, :].astype(f32)
                grads = gprobs[part, :]
                grads = prob * (grads - jnp.sum(grads * prob, axis=-1, keepdims=True))
                gscores[part, :] = (grads * scale).astype(bf16)
                if c == 0:
                    bias[lev * HEADS + group * GROUP + h] = grads
                else:
                    bias[lev * HEADS + group * GROUP + h] += grads
            gproj_ref[rows, at(group + 4, GWIDTH)] = dot_tn(probs_ref[probs], upstream).astype(bf16)
            query = head_stack(proj_ref[rows, at(group, GWIDTH)])
            gproj_ref[rows, at(group + 2, GWIDTH)] = dot_tn(gscores[...], query).astype(bf16)
            gquery = dot(gscores[...], proj_ref[rows, at(group + 2, GWIDTH)])
            gproj_ref[rows, at(group, GWIDTH)] = head_join(gquery).astype(bf16)

    loop(4, back)

    def share(i):
        head = lax.rem(place_ref[1] + i // 2, 4) * 2 + lax.rem(i, 2)
        keep_ref[i] = bias[place_ref[0] * HEADS + head].astype(bf16)
        send_ref[i] = bias[(1 - place_ref[0]) * HEADS + head].astype(bf16)

    loop(HEADS, share)


def qkv_grad_kernel(place_ref, tok_ref, gproj_ref, keep_ref, send_ref, normed, wgrad):
    def norm_rows(i):
        values, _ = normalize(tok_ref[at(i, 48), :].astype(f32))
        normed[at(i, 48), :] = values.astype(bf16)

    loop(TOKENS // 48, norm_rows)

    def product(i):
        wgrad[:, at(i, 512)] = dot_tn(normed[...], gproj_ref[:, at(i, 512)])

    loop(3, product)

    def share(i):
        dy, dx = i // 4, lax.rem(i, 4)
        for other, ref in ((False, keep_ref), (True, send_ref)):
            ref[at(i, 16), :] = wgrad[at(chunk_id(dy, dx, 0, place_ref, other), 16), :].astype(bf16)

    loop(16, share)


def token_grad_kernel(tok_ref, gproj_ref, qkv_ref, gresid_ref, spread_ref, pieces_ref, back, result):
    def product(i):
        back[:, at(i, 256)] = dot_nt(gproj_ref[...], qkv_ref[at(i, 256), :])

    loop(2, product)

    def norm_rows(i):
        rows = at(i, 48)
        values, inv_std = normalize(tok_ref[rows, :].astype(f32))
        result[rows, :] = (gresid_ref[rows, :] + norm_back(values, inv_std, back[rows, :])).astype(bf16)

    loop(TOKENS // 48, norm_rows)
    pieces_ref[...] = dot(spread_ref[...], result[...]).astype(bf16)


def call(kernel, outs, scratch, flops, *operands):
    shapes = [jax.ShapeDtypeStruct(shape, dtype) for shape, dtype in outs]
    specs = [
        pl.BlockSpec(memory_space=pltpu.SMEM if operand.dtype == jnp.int32 else pltpu.VMEM)
        for operand in operands
    ]
    return pl.pallas_call(
        kernel,
        out_shape=shapes,
        in_specs=specs,
        out_specs=[pl.BlockSpec(memory_space=pltpu.VMEM)] * len(outs),
        scratch_shapes=[pltpu.VMEM(shape, dtype) for shape, dtype in scratch],
        compiler_params=pltpu.CompilerParams(vmem_limit_bytes=50 * 2**20),
        cost_estimate=pl.CostEstimate(flops=flops, bytes_accessed=2**20, transcendentals=2**20),
    )(*operands)


def device_index(z, x, y, core):
    return z * 32 + (x % 2) * 16 + (x // 2) * 8 + y * 2 + core


def permute(value, move):
    pairs = []
    for z in range(4):
        for x in range(4):
            for y in range(4):
                for core in range(2):
                    pairs.append((device_index(z, x, y, core), device_index(*move(z, x, y, core))))
    return lax.ppermute(value, ("lat", "lon"), pairs)


def to_core(value):
    return permute(value, lambda z, x, y, core: (z, x, y, 1 - core))


def to_y(value, by):
    return permute(value, lambda z, x, y, core: (z, x, (y + by) % 4, core))


def to_x(value, by):
    return permute(value, lambda z, x, y, core: (z, (x + by) % 4, y, core))


def to_z(value, by):
    return permute(value, lambda z, x, y, core: ((z + by) % 4, x, y, core))


def to_half(value):
    return permute(value, lambda z, x, y, core: (z, (x + 2) % 4, y, core))


def shift(value, lat_by, lon_by):
    pairs = []
    for lat in range(8):
        for lon in range(16):
            pairs.append((lat * 16 + lon, (lat + lat_by) % 8 * 16 + (lon + lon_by) % 16))
    return lax.ppermute(value, ("lat", "lon"), pairs)


def total_of(parts):
    total = parts[0].astype(f32)
    for part in parts[1:]:
        total = total + part.astype(f32)
    return total


def cut(value, parts):
    size = value.shape[0] // parts
    return [value[i * size : (i + 1) * size] for i in range(parts)]


def sum_over_plane(keep, send):
    mine = [total_of(pair).astype(bf16) for pair in zip(cut(keep, 4), cut(to_core(send), 4))]
    mine = cut(total_of([mine[0]] + [to_y(mine[by], by) for by in (1, 2, 3)]).astype(bf16), 4)
    return total_of([mine[0]] + [to_x(mine[by], by) for by in (1, 2, 3)]).astype(bf16)


def halos(field):
    band = field[:, :HALF_LAT].reshape(BAND, WIDTH)
    side = field[:, HALF_LAT:, :EDGE].reshape(SIDE, WIDTH)
    corner = field[:, :HALF_LAT, :EDGE].reshape(SIDE, WIDTH)
    return [shift(band, -1, 0), shift(side, 0, -1), shift(corner, -1, -1)]


def give_back(pieces):
    stay = pieces[:BAND].reshape(LEVELS, HALF_LAT, COLS, WIDTH)
    band = shift(pieces[BAND : 2 * BAND], 1, 0).reshape(LEVELS, HALF_LAT, COLS, WIDTH)
    side = shift(pieces[2 * BAND : 2 * BAND + SIDE], 0, 1).reshape(LEVELS, HALF_LAT, EDGE, WIDTH)
    corner = shift(pieces[2 * BAND + SIDE :], 1, 1).reshape(LEVELS, HALF_LAT, EDGE, WIDTH)
    wider = ((0, 0), (0, 0), (0, COLS - EDGE), (0, 0))
    return jnp.concatenate([band + jnp.pad(corner, wider), stay + jnp.pad(side, wider)], axis=1)


def masked_bias(earth_bias):
    token = jnp.arange(WTOK, dtype=jnp.int32)
    wrap_lev = (token >= WTOK // 2).astype(jnp.int32)
    wrap_row = (token % (WTOK // 2) >= HALF_LAT * WIN_LON).astype(jnp.int32)
    wrap_row = wrap_row * (lax.axis_index("lat") == lax.axis_size("lat") - 1).astype(jnp.int32)
    codes = jnp.stack([wrap_row, 2 * wrap_lev + wrap_row])
    allowed = codes[:, :, None] == codes[:, None, :]
    bias = earth_bias.reshape(2, HEADS, WTOK, WTOK)
    return jnp.where(allowed[:, None], bias, masked_score).reshape(2 * HEADS, WTOK, WTOK)


def body(latent, cotangent, qkv_weight, out_weight, up_weight, down_weight, earth_bias):
    lat, lon = lax.axis_index("lat"), lax.axis_index("lon")
    core, y = lon % 2, (lon // 2) % 4
    x, z = (lon // 8) * 2 + lat % 2, lat // 2
    place = jnp.stack([core, y, x]).astype(jnp.int32)
    pick_table, spread_table = token_tables()
    pick, spread = jnp.asarray(pick_table), jnp.asarray(spread_table)

    near = halos(latent)
    later, near[0] = lax.optimization_barrier((cotangent, near[0]))
    grad_near = halos(later)
    tok, proj, probs, mixed = call(
        attend_kernel,
        [((TOKENS, WIDTH), bf16), ((TOKENS, 3 * WIDTH), bf16), ((8, GTOK, WTOK), bf16), ((TOKENS, WIDTH), bf16)],
        [((TOKENS + BAND + 2 * SIDE, WIDTH), bf16), ((TOKENS, WIDTH), bf16), ((GTOK, WTOK), f32)],
        4 * 10**9,
        pick, latent.reshape(TOKENS, WIDTH), *near, masked_bias(earth_bias), qkv_weight,
    )
    pieces, gresid, keep, send = call(
        mlp_kernel,
        [
            ((2 * BAND + 2 * SIDE, WIDTH), bf16), ((TOKENS, WIDTH), f32),
            ((48 * CHUNK, WIDTH), bf16), ((48 * CHUNK, WIDTH), bf16),
        ],
        [
            ((TOKENS + BAND + 2 * SIDE, WIDTH), bf16), ((TOKENS, WIDTH), bf16), ((TOKENS, WIDTH), f32),
            ((TOKENS, WIDTH), f32), ((TOKENS, WIDTH), bf16), ((TOKENS, 128), f32),
            ((TOKENS, WIDTH), f32), ((TOKENS, WIDTH), f32),
            ((TOKENS, HIDDEN), bf16), ((TOKENS, HIDDEN), bf16), ((TOKENS, WIDTH), bf16),
            ((4, 9 * WIDTH, 128), f32),
        ],
        8 * 10**9,
        place, pick, spread, cotangent.reshape(TOKENS, WIDTH), *grad_near, tok, mixed,
        out_weight, up_weight, down_weight,
    )
    gproj, bias_keep, bias_send = call(
        attend_back_kernel,
        [((TOKENS, 3 * WIDTH), bf16), ((HEADS, WTOK, WTOK), bf16), ((HEADS, WTOK, WTOK), bf16)],
        [((TOKENS, WIDTH), bf16), ((GTOK, WTOK), f32), ((GTOK, WTOK), bf16), ((2 * HEADS, WTOK, WTOK), f32)],
        6 * 10**9,
        place, proj, probs, gresid, out_weight,
    )
    qkv_keep, qkv_send = call(
        qkv_grad_kernel,
        [((256, 3 * WIDTH), bf16), ((256, 3 * WIDTH), bf16)],
        [((TOKENS, WIDTH), bf16), ((WIDTH, 3 * WIDTH), f32)],
        2 * 10**9,
        place, tok, gproj,
    )
    (grad_pieces,) = call(
        token_grad_kernel,
        [((2 * BAND + 2 * SIDE, WIDTH), bf16)],
        [((TOKENS, WIDTH), f32), ((TOKENS, WIDTH), bf16)],
        2 * 10**9,
        tok, gproj, qkv_weight, gresid, spread,
    )
    out = give_back(pieces)
    grad_latent = give_back(grad_pieces)

    others = sum_over_plane(keep, send).reshape(3, CHUNK, WIDTH)
    first = sum_over_plane(qkv_keep, qkv_send).reshape(1, CHUNK, WIDTH)
    shares = jnp.concatenate([first, others])
    ahead = [lax.dynamic_index_in_dim(shares, (z + by) % 4, 0, False) for by in range(4)]
    total = total_of([ahead[0]] + [to_z(ahead[by], by) for by in (1, 2, 3)])
    weight_grad = total.reshape(-1) * (1.0 / math.sqrt(TOKENS * lax.axis_size("lat") * lax.axis_size("lon")))

    mine = [total_of(pair).astype(bf16) for pair in zip(cut(bias_keep, 4), cut(to_core(bias_send), 4))]
    mine = total_of([mine[0]] + [to_y(mine[by], by) for by in (1, 2, 3)]).astype(bf16)
    mine = total_of([mine, to_half(mine)]).astype(bf16)
    ring = [mine] + [to_y(mine, -by) for by in (1, 2, 3)]
    ring = jnp.stack(ring + ring)
    half = lax.dynamic_slice_in_dim(ring, (4 - y) % 4, 4, 0).reshape(1, HEADS, WTOK, WTOK)
    other = to_core(half)
    both = jnp.where(core == 0, jnp.concatenate([half, other]), jnp.concatenate([other, half]))
    bias_grad = both.astype(f32).reshape(1, 2, HEADS, WTOK * WTOK)
    return (out, grad_latent, weight_grad, bias_grad)


def solution(mesh):
    field = P(None, "lat", "lon", None)
    band = P("lat", None, None, None)
    in_specs = (field, field, P(), P(), P(), P(), band)
    out_specs = (field, field, P(("lat", "lon")), band)
    return jax.shard_map(body, mesh=mesh, in_specs=in_specs, out_specs=out_specs, check_vma=False)
```

time: 501 us -> 195 us (0.39)
  waiting for transfers between devices: 269 us -> 61 us
  local copies, waits for them, and re-layouts: 115 us -> 11.2 us
  Pallas kernels: 0 us -> 62.5 us
  matrix products: 56 us -> 0 us
  starting transfers between devices: 9.8 us -> 44.9 us
  other arithmetic: 31.9 us -> 13.3 us
  between operations: 14.8 us -> 1.08 us
    unnamed x3 -> x0, waiting for transfers between devices: 168 us -> none
    psum x1 -> x0, waiting for transfers between devices: 80.3 us -> none  [body(): lax.psum(grad_bias.astype(jnp.bfloat16), 'lon').astype(jnp.float32)]
    pallas_call x0 -> x5, Pallas kernels: none -> 62.5 us  [call(): pl.pallas_call(kernel, out_shape=shapes, in_specs=specs, out_specs=[pl.Bl...]
    dot_general x18 -> x0, matrix products: 56 us -> none  [the longest x12 32.5 us: matmul(): return jnp.dot(left, right, preferred_element_type=jnp.float32)]
    ppermute x4 -> x38, waiting for transfers between devices: 20.8 us -> 61 us  [the longest x26 56.8 us: permute(): return lax.ppermute(value, ('lat', 'lon'), pairs)]
    ppermute x4 -> x38, starting transfers between devices: 9.72 us -> 44.9 us  [the longest x26 26.1 us: permute(): return lax.ppermute(value, ('lat', 'lon'), pairs)]
    reshape x13 -> x2, local copies, waits for them, and re-layouts: 39.1 us -> 4.5 us  [the longest x1 4.47 us: masked_bias(): bias = earth_bias.reshape(2, HEADS, WTOK, WTOK)]
    unnamed x61 -> x21, local copies, waits for them, and re-layouts: 20.5 us -> 1.97 us
  transfers between devices with their start and end apart: 6 -> 38, of which waited for: 4 -> 18; matrix products, arithmetic and copies ran while one was open for 12% -> 11% of each run, Pallas kernels for 0% -> 10%
where the time goes in v1:
time: 195 us; the launch traced here: 194 us
  Pallas kernels  62.5 us (32%)
  waiting for transfers between devices  61 us (31%)
  starting transfers between devices  44.9 us (23%)
  other arithmetic  13.3 us (7%)
  local copies, waits for them, and re-layouts  11.2 us (6%)
    pallas_call x5, Pallas kernels, call(): pl.pallas_call(kernel, out_shape=shapes, in_specs=specs, out_specs=[pl.Bl...  62.5 us
    ppermute x26, waiting for transfers between devices, permute(): return lax.ppermute(value, ('lat', 'lon'), pairs)  56.8 us
    ppermute x26, starting transfers between devices, permute(): return lax.ppermute(value, ('lat', 'lon'), pairs)  26.1 us
    ppermute x12, starting transfers between devices, shift(): return lax.ppermute(value, ('lat', 'lon'), pairs)  18.8 us
    reshape x1, local copies, waits for them, and re-layouts, masked_bias(): bias = earth_bias.reshape(2, HEADS, WTOK, WTOK)  4.47 us
    ppermute x12, waiting for transfers between devices, shift(): return lax.ppermute(value, ('lat', 'lon'), pairs)  4.28 us
  transfers between devices with their start and end apart: 38, of which 18 were waited for; matrix products, arithmetic and copies ran while one was open for 11% of the time, Pallas kernels for 10%

profile of v1, /device:TPU:1, one launch (start us, length us, event | category | flops | bytes accessed | tf_op | source)
XLA Modules:
  0.0 194.0 jit_solution(1117652741409581375)
XLA Ops:
  0.6 1.0 slice.138
  1.6 5.6 %collective-permute-start = (bf16[288,512]{1,0:T(8,128)(2,1)S(1)}, bf16[288,512]{1,0:T(8,128)(2,1)S(1)}, u32[]{:S(2)}, u32[]{:S(2)}) collective-permute-start(bf16[288,512]{1,0:T(8,128)(2,1)S(1)} %bitcast.62), channel_id=1, source_target_pairs={{0,112},{1,113},{2,114},{3,115},{4,116},{5,117},{6,118},{7,119},{8... | collective-permute-start | bytes 884744 | tf_op jit(solution)/shard_map/ppermute | solution.py:371
  7.2 1.0 fusion.19
  8.2 1.0 collective-permute-start.4
  9.2 4.2 %collective-permute-start.5 = (bf16[96,512]{1,0:T(8,128)(2,1)S(1)}, bf16[96,512]{1,0:T(8,128)(2,1)S(1)}, u32[]{:S(2)}, u32[]{:S(2)}) collective-permute-start(bf16[96,512]{1,0:T(8,128)(2,1)S(1)} %bitcast.67), channel_id=1, source_target_pairs={{0,127},{1,112},{2,113},{3,114},{4,115},{5,116},{6,117},{7,118},{8... | collective-permute-start | bytes 294920 | tf_op jit(solution)/shard_map/ppermute | solution.py:371
  13.4 4.5 %reshape.189 = f32[16,144,144]{2,1,0:T(8,128)} reshape(f32[1,2,8,20736]{3,2,1,0:T(8,128)} %param.15) | data formatting | bytes 2654208 | tf_op jit(solution)/shard_map/reshape | solution.py:415
  18.0 3.5 %bitcast_select_fusion.bias_ref = f32[16,144,144]{2,1,0:T(8,128)} fusion(f32[16,144,144]{2,1,0:T(8,128)} %reshape.189, pred[2,144,144]{2,1,0:T(8,128)(4,1)S(1)} %broadcast_compare_fusion), kind=kLoop, calls=%fused_computation | loop fusion | flops 331776 | bytes 2695680 | tf_op jit(solution)/shard_map/jit(_where)/select_n | solution.py:416
  21.7 1.4 collective-permute-start.1
  24.0 14.3 %shard_map.120 = (bf16[576,512]{1,0:T(8,128)(2,1)S(1)}, bf16[576,1536]{1,0:T(8,128)(2,1)}, bf16[8,576,144]{2,1,0:T(8,128)(2,1)}, bf16[576,512]{1,0:T(8,128)(2,1)S(1)}) custom-call(bf16[576,1056]{1,0:T(8,128)(2,1)S(1)} %copy-done.3, bf16[576,512]{1,0:T(8,128)(2,1)S(1)} %bitcast.55, bf16[288,512]{1,0:T(8,128)(2,1)S(1)} %collective-permute-done.row_ref, ...), custom_call_target="tpu_custom_call" | custom-call | flops 4000000000 | bytes 1048576 | tf_op jit(solution)/shard_map/pallas_call | solution.py:321
  38.4 26.1 %shard_map.121 = (bf16[768,512]{1,0:T(8,128)(2,1)S(1)}, f32[576,512]{1,0:T(8,128)}, bf16[2304,512]{1,0:T(8,128)(2,1)}, bf16[2304,512]{1,0:T(8,128)(2,1)}) custom-call(s32[3]{0:T(128)S(1)} %pad_add_fusion.5.place_ref, bf16[576,1056]{1,0:T(8,128)(2,1)} %constant.126.clone.pick_ref, bf16[768,576]{1,0:T(8,128)(2,1)} %constant.127.clone.spread_ref, ...), custom_call_target="tpu_custom_call" | custom-call | flops 8000000000 | bytes 1048576 | tf_op jit(solution)/shard_map/pallas_call | solution.py:321
  64.6 1.2 copy-done.6
  65.8 9.6 %shard_map.122 = (bf16[576,1536]{1,0:T(8,128)(2,1)}, bf16[8,144,144]{2,1,0:T(8,128)(2,1)S(1)}, bf16[8,144,144]{2,1,0:T(8,128)(2,1)S(1)}) custom-call(s32[3]{0:T(128)S(1)} %pad_add_fusion.5.place_ref, bf16[576,1536]{1,0:T(8,128)(2,1)} %get-tuple-element.24.proj_ref, bf16[8,576,144]{2,1,0:T(8,128)(2,1)} %get-tuple-element.25.probs_ref, ...), custom_call_target="tpu_custom_call" | custom-call | flops 6000000000 | bytes 1048576 | tf_op jit(solution)/shard_map/pallas_call | solution.py:321
  75.3 7.4 %shard_map.123 = bf16[768,512]{1,0:T(8,128)(2,1)S(1)} custom-call(bf16[576,512]{1,0:T(8,128)(2,1)S(1)} %get-tuple-element.21.tok_ref, bf16[576,1536]{1,0:T(8,128)(2,1)} %get-tuple-element.27.gproj_ref, bf16[512,1536]{1,0:T(8,128)(2,1)} %qkv_ref.3, f32[576,512]{1,0:T(8,128)S(1)} %copy-done.6, bf16[768,576]{1,0:T(8,128)(2,1)S(1)} %copy-done.4), custom_call_target="tpu_custom_call" | custom-call | flops 2000000000 | bytes 1048576 | tf_op jit(solution)/shard_map/pallas_call | solution.py:321
  82.8 1.4 collective-permute-start.8
  84.9 1.9 collective-permute-start.7
  86.8 1.4 collective-permute-start.9
  88.2 5.0 %shard_map.124 = (bf16[256,1536]{1,0:T(8,128)(2,1)S(1)}, bf16[256,1536]{1,0:T(8,128)(2,1)S(1)}) custom-call(s32[3]{0:T(128)S(1)} %pad_add_fusion.5.place_ref, bf16[576,512]{1,0:T(8,128)(2,1)S(1)} %get-tuple-element.21.tok_ref, bf16[576,1536]{1,0:T(8,128)(2,1)S(1)} %copy-done.5), custom_call_target="tpu_custom_call" | custom-call | flops 2000000000 | bytes 1048576 | tf_op jit(solution)/shard_map/pallas_call | solution.py:321
  93.6 7.5 %collective-permute-start.29 = (bf16[8,144,144]{2,1,0:T(8,128)(2,1)S(1)}, bf16[8,144,144]{2,1,0:T(8,128)(2,1)S(1)}, u32[]{:S(2)}, u32[]{:S(2)}) collective-permute-start(bf16[8,144,144]{2,1,0:T(8,128)(2,1)S(1)} %get-tuple-element.33), channel_id=1, source_target_pairs={{0,1},{1,0},{2,3},{3,2},{4,5},{5,4},{6,7},{7,6},{16,17},{17,16},{1... | collective-permute-start | bytes 995336 | tf_op jit(solution)/shard_map/ppermute | solution.py:343
  101.8 1.0 collective-permute-done.29
  103.0 4.3 %collective-permute-done.10 = bf16[96,512]{1,0:T(8,128)(2,1)S(1)} collective-permute-done((bf16[96,512]{1,0:T(8,128)(2,1)S(1)}, bf16[96,512]{1,0:T(8,128)(2,1)S(1)}, u32[]{:S(2)}, u32[]{:S(2)}) %collective-permute-start.10) | collective-permute-done | bytes 98336 | tf_op jit(solution)/shard_map/ppermute | solution.py:371
  108.0 4.8 %collective-permute-done.31 = bf16[2,144,144]{2,1,0:T(8,128)(2,1)S(1)} collective-permute-done((bf16[2,144,144]{2,1,0:T(8,128)(2,1)S(1)}, bf16[2,144,144]{2,1,0:T(8,128)(2,1)S(1)}, u32[]{:S(2)}, u32[]{:S(2)}) %collective-permute-start.31) | collective-permute-done | bytes 82976 | tf_op jit(solution)/shard_map/ppermute | solution.py:343
  112.8 2.6 %collective-permute-done.30 = bf16[2,144,144]{2,1,0:T(8,128)(2,1)S(1)} collective-permute-done((bf16[2,144,144]{2,1,0:T(8,128)(2,1)S(1)}, bf16[2,144,144]{2,1,0:T(8,128)(2,1)S(1)}, u32[]{:S(2)}, u32[]{:S(2)}) %collective-permute-start.30) | collective-permute-done | bytes 82976 | tf_op jit(solution)/shard_map/ppermute | solution.py:343
  115.5 1.0 collective-permute-start.33
  117.4 4.3 %collective-permute-done.33 = bf16[2,144,144]{2,1,0:T(8,128)(2,1)S(1)} collective-permute-done((bf16[2,144,144]{2,1,0:T(8,128)(2,1)S(1)}, bf16[2,144,144]{2,1,0:T(8,128)(2,1)S(1)}, u32[]{:S(2)}, u32[]{:S(2)}) %collective-permute-start.33) | collective-permute-done | bytes 82976 | tf_op jit(solution)/shard_map/ppermute | solution.py:343
  122.6 2.8 %collective-permute-start.35 = (bf16[2,144,144]{2,1,0:T(8,128)(2,1)S(1)}, bf16[2,144,144]{2,1,0:T(8,128)(2,1)S(1)}, u32[]{:S(2)}, u32[]{:S(2)}) collective-permute-start(bf16[2,144,144]{2,1,0:T(8,128)(2,1)S(1)} %get-tuple-element.35), channel_id=1, source_target_pairs={{0,4},{1,5},{2,6},{3,7},{4,0},{5,1},{6,2},{7,3},{16,20},{17,21},{1... | collective-permute-start | bytes 248840 | tf_op jit(solution)/shard_map/ppermute | solution.py:343
  126.3 1.9 collective-permute-done.35
  128.2 4.7 %collective-permute-done.36 = bf16[2,144,144]{2,1,0:T(8,128)(2,1)S(1)} collective-permute-done((bf16[2,144,144]{2,1,0:T(8,128)(2,1)S(1)}, bf16[2,144,144]{2,1,0:T(8,128)(2,1)S(1)}, u32[]{:S(2)}, u32[]{:S(2)}) %collective-permute-start.36) | collective-permute-done | bytes 82976 | tf_op jit(solution)/shard_map/ppermute | solution.py:343
  133.7 1.7 collective-permute-start.37
  135.4 0.9 add_convert_fusion.8
  136.3 2.2 %collective-permute-start.14 = (bf16[64,1536]{1,0:T(8,128)(2,1)}, bf16[64,1536]{1,0:T(8,128)(2,1)}, u32[]{:S(2)}, u32[]{:S(2)}) collective-permute-start(bf16[64,1536]{1,0:T(8,128)(2,1)} %get-tuple-element.41), channel_id=1, source_target_pairs={{0,4},{1,5},{2,6},{3,7},{4,0},{5,1},{6,2},{7,3},{16,20},{17,21},{1... | collective-permute-start | bytes 589832 | tf_op jit(solution)/shard_map/ppermute | solution.py:343
  138.7 1.8 concatenate.37
  140.5 2.5 %add_convert_fusion.3 = (bf16[576,512]{1,0:T(8,128)(2,1)S(1)}, bf16[576,512]{1,0:T(8,128)(2,1)S(1)}, bf16[576,512]{1,0:T(8,128)(2,1)S(1)}) fusion(bf16[2304,512]{1,0:T(8,128)(2,1)} %collective-permute-done.19, bf16[2304,512]{1,0:T(8,128)(2,1)} %get-tuple-element.30), kind=kLoop, calls=%fused_computation.4 | loop fusion | flops 3538944 | bytes 5308416 | tf_op jit(solution)/shard_map/convert_element_type | solution.py:387
  143.0 2.5 %collective-permute-start.22 = (bf16[576,512]{1,0:T(8,128)(2,1)S(1)}, bf16[576,512]{1,0:T(8,128)(2,1)S(1)}, u32[]{:S(2)}, u32[]{:S(2)}) collective-permute-start(bf16[576,512]{1,0:T(8,128)(2,1)S(1)} %get-tuple-element.37), channel_id=1, source_target_pairs={{0,6},{1,7},{2,0},{3,1},{4,2},{5,3},{6,4},{7,5},{16,22},{17,23},{1... | collective-permute-start | bytes 1769480 | tf_op jit(solution)/shard_map/ppermute | solution.py:343
  146.5 2.6 %collective-permute-done.13 = bf16[64,1536]{1,0:T(8,128)(2,1)} collective-permute-done((bf16[64,1536]{1,0:T(8,128)(2,1)S(1)}, bf16[64,1536]{1,0:T(8,128)(2,1)}, u32[]{:S(2)}, u32[]{:S(2)}) %collective-permute-start.13) | collective-permute-done | bytes 196640 | tf_op jit(solution)/shard_map/ppermute | solution.py:343
  149.1 1.1 add_convert_fusion.5
  150.4 2.5 %collective-permute-start.17 = (bf16[16,1536]{1,0:T(8,128)(2,1)S(1)}, bf16[16,1536]{1,0:T(8,128)(2,1)S(1)}, u32[]{:S(2)}, u32[]{:S(2)}) collective-permute-start(bf16[16,1536]{1,0:T(8,128)(2,1)S(1)} %get-tuple-element.65), channel_id=1, source_target_pairs={{0,8},{1,9},{2,10},{3,11},{4,12},{5,13},{6,14},{7,15},{16,24},{17,... | collective-permute-start | bytes 147464 | tf_op jit(solution)/shard_map/ppermute | solution.py:343
  152.9 7.0 %collective-permute-done.22 = bf16[576,512]{1,0:T(8,128)(2,1)S(1)} collective-permute-done((bf16[576,512]{1,0:T(8,128)(2,1)S(1)}, bf16[576,512]{1,0:T(8,128)(2,1)S(1)}, u32[]{:S(2)}, u32[]{:S(2)}) %collective-permute-start.22) | collective-permute-done | bytes 589856 | tf_op jit(solution)/shard_map/ppermute | solution.py:343
  159.9 0.9 collective-permute-done.21
  160.8 14.1 %collective-permute-done.20 = bf16[576,512]{1,0:T(8,128)(2,1)S(1)} collective-permute-done((bf16[576,512]{1,0:T(8,128)(2,1)S(1)}, bf16[576,512]{1,0:T(8,128)(2,1)S(1)}, u32[]{:S(2)}, u32[]{:S(2)}) %collective-permute-start.20) | collective-permute-done | bytes 589856 | tf_op jit(solution)/shard_map/ppermute | solution.py:343
  174.8 1.6 add_convert_fusion
  176.6 1.2 collective-permute-start.24
  178.2 3.3 %collective-permute-done.25 = bf16[144,512]{1,0:T(8,128)(2,1)S(1)} collective-permute-done((bf16[144,512]{1,0:T(8,128)(2,1)S(1)}, bf16[144,512]{1,0:T(8,128)(2,1)S(1)}, u32[]{:S(2)}, u32[]{:S(2)}) %collective-permute-start.25) | collective-permute-done | bytes 147488 | tf_op jit(solution)/shard_map/ppermute | solution.py:343
  181.5 1.6 collective-permute-done.24
  183.1 4.0 %collective-permute-done.23 = bf16[144,512]{1,0:T(8,128)(2,1)S(1)} collective-permute-done((bf16[144,512]{1,0:T(8,128)(2,1)S(1)}, bf16[144,512]{1,0:T(8,128)(2,1)S(1)}, u32[]{:S(2)}, u32[]{:S(2)}) %collective-permute-start.23) | collective-permute-done | bytes 147488 | tf_op jit(solution)/shard_map/ppermute | solution.py:343
  187.3 1.2 collective-permute-start.27
  188.7 1.2 fusion
  190.2 1.6 collective-permute-done.27
  191.8 1.5 collective-permute-done.26
  (93 shorter events, 10.9 us)
Async XLA Ops:
  1.6 20.0 %collective-permute-start = (bf16[288,512]{1,0:T(8,128)(2,1)S(1)}, bf16[288,512]{1,0:T(8,128)(2,1)S(1)}, u32[]{:S(2)}, u32[]{:S(2)}) collective-permute-start(bf16[288,512]{1,0:T(8,128)(2,1)S(1)} %bitcast.62), channel_id=1, source_target_pairs={{0,112},{1,113},{2,114},{3,115},{4,116},{5,117},{6,118},{7,119},{8... | collective-permute-start | bytes 884744 | tf_op jit(solution)/shard_map/ppermute | solution.py:371
  8.2 15.8 %collective-permute-start.4 = (bf16[96,512]{1,0:T(8,128)(2,1)S(1)}, bf16[96,512]{1,0:T(8,128)(2,1)S(1)}, u32[]{:S(2)}, u32[]{:S(2)}) collective-permute-start(bf16[96,512]{1,0:T(8,128)(2,1)S(1)} %bitcast.68), channel_id=1, source_target_pairs={{0,15},{1,0},{2,1},{3,2},{4,3},{5,4},{6,5},{7,6},{8,7},{9,8},{10,9... | collective-permute-start | bytes 294920 | tf_op jit(solution)/shard_map/ppermute | solution.py:371
  9.2 14.8 %collective-permute-start.5 = (bf16[96,512]{1,0:T(8,128)(2,1)S(1)}, bf16[96,512]{1,0:T(8,128)(2,1)S(1)}, u32[]{:S(2)}, u32[]{:S(2)}) collective-permute-start(bf16[96,512]{1,0:T(8,128)(2,1)S(1)} %bitcast.67), channel_id=1, source_target_pairs={{0,127},{1,112},{2,113},{3,114},{4,115},{5,116},{6,117},{7,118},{8... | collective-permute-start | bytes 294920 | tf_op jit(solution)/shard_map/ppermute | solution.py:371
  18.0 3.6 %copy-start.1 = (bf16[4,6,24,512]{3,2,1,0:T(8,128)(2,1)S(1)}, bf16[4,6,24,512]{3,2,1,0:T(8,128)(2,1)}, u32[]{:S(2)}) copy-start(bf16[4,6,24,512]{3,2,1,0:T(8,128)(2,1)} %param.10) | copy-start | bytes 1769476
  18.0 6.0 %copy-start = (bf16[4,6,24,512]{3,2,1,0:T(8,128)(2,1)S(1)}, bf16[4,6,24,512]{3,2,1,0:T(8,128)(2,1)}, u32[]{:S(2)}) copy-start(bf16[4,6,24,512]{3,2,1,0:T(8,128)(2,1)} %param.9) | copy-start | bytes 1769476
  18.0 6.0 %copy-start.3 = (bf16[576,1056]{1,0:T(8,128)(2,1)S(1)}, bf16[576,1056]{1,0:T(8,128)(2,1)}, u32[]{:S(2)}) copy-start(bf16[576,1056]{1,0:T(8,128)(2,1)} %constant.126.clone.pick_ref) | copy-start | bytes 3649540
  21.7 16.7 %collective-permute-start.1 = (bf16[288,512]{1,0:T(8,128)(2,1)S(1)}, bf16[288,512]{1,0:T(8,128)(2,1)S(1)}, u32[]{:S(2)}, u32[]{:S(2)}) collective-permute-start(bf16[288,512]{1,0:T(8,128)(2,1)S(1)} %bitcast.63), channel_id=1, source_target_pairs={{0,112},{1,113},{2,114},{3,115},{4,116},{5,117},{6,118},{7,119},{8... | collective-permute-start | bytes 884744 | tf_op jit(solution)/shard_map/ppermute | solution.py:371
  23.1 15.2 %collective-permute-start.2 = (bf16[96,512]{1,0:T(8,128)(2,1)S(1)}, bf16[96,512]{1,0:T(8,128)(2,1)S(1)}, u32[]{:S(2)}, u32[]{:S(2)}) collective-permute-start(bf16[96,512]{1,0:T(8,128)(2,1)S(1)} %bitcast.70), channel_id=1, source_target_pairs={{0,15},{1,0},{2,1},{3,2},{4,3},{5,4},{6,5},{7,6},{8,7},{9,8},{10,9... | collective-permute-start | bytes 294920 | tf_op jit(solution)/shard_map/ppermute | solution.py:371
  23.1 15.2 %collective-permute-start.3 = (bf16[96,512]{1,0:T(8,128)(2,1)S(1)}, bf16[96,512]{1,0:T(8,128)(2,1)S(1)}, u32[]{:S(2)}, u32[]{:S(2)}) collective-permute-start(bf16[96,512]{1,0:T(8,128)(2,1)S(1)} %bitcast.69), channel_id=1, source_target_pairs={{0,127},{1,112},{2,113},{3,114},{4,115},{5,116},{6,117},{7,118},{8... | collective-permute-start | bytes 294920 | tf_op jit(solution)/shard_map/ppermute | solution.py:371
  24.0 14.4 %copy-start.2 = (bf16[512,512]{1,0:T(8,128)(2,1)S(1)}, bf16[512,512]{1,0:T(8,128)(2,1)}, u32[]{:S(2)}) copy-start(bf16[512,512]{1,0:T(8,128)(2,1)} %out_ref.3) | copy-start | bytes 1572868
  64.5 1.3 copy-start.6
  65.8 9.6 %copy-start.4 = (bf16[768,576]{1,0:T(8,128)(2,1)S(1)}, bf16[768,576]{1,0:T(8,128)(2,1)}, u32[]{:S(2)}) copy-start(bf16[768,576]{1,0:T(8,128)(2,1)} %constant.127.clone.spread_ref) | copy-start | bytes 2654212
  75.3 12.8 %copy-start.5 = (bf16[576,1536]{1,0:T(8,128)(2,1)S(1)}, bf16[576,1536]{1,0:T(8,128)(2,1)}, u32[]{:S(2)}) copy-start(bf16[576,1536]{1,0:T(8,128)(2,1)} %get-tuple-element.27.gproj_ref) | copy-start | bytes 5308420
  82.8 10.4 %collective-permute-start.8 = (bf16[96,512]{1,0:T(8,128)(2,1)S(1)}, bf16[96,512]{1,0:T(8,128)(2,1)S(1)}, u32[]{:S(2)}, u32[]{:S(2)}) collective-permute-start(bf16[96,512]{1,0:T(8,128)(2,1)S(1)} %get-tuple-element.50), channel_id=1, source_target_pairs={{0,1},{1,2},{2,3},{3,4},{4,5},{5,6},{6,7},{7,8},{8,9},{9,10},{10,1... | collective-permute-start | bytes 294920 | tf_op jit(solution)/shard_map/ppermute | solution.py:371
  84.2 17.1 %collective-permute-start.6 = (bf16[288,512]{1,0:T(8,128)(2,1)S(1)}, bf16[288,512]{1,0:T(8,128)(2,1)S(1)}, u32[]{:S(2)}, u32[]{:S(2)}) collective-permute-start(bf16[288,512]{1,0:T(8,128)(2,1)S(1)} %get-tuple-element.51), channel_id=1, source_target_pairs={{0,16},{1,17},{2,18},{3,19},{4,20},{5,21},{6,22},{7,23},{8,24},{9,... | collective-permute-start | bytes 884744 | tf_op jit(solution)/shard_map/ppermute | solution.py:371
  84.9 16.2 %collective-permute-start.7 = (bf16[96,512]{1,0:T(8,128)(2,1)S(1)}, bf16[96,512]{1,0:T(8,128)(2,1)S(1)}, u32[]{:S(2)}, u32[]{:S(2)}) collective-permute-start(bf16[96,512]{1,0:T(8,128)(2,1)S(1)} %get-tuple-element.49), channel_id=1, source_target_pairs={{0,17},{1,18},{2,19},{3,20},{4,21},{5,22},{6,23},{7,24},{8,25},{9,... | collective-permute-start | bytes 294920 | tf_op jit(solution)/shard_map/ppermute | solution.py:371
  86.8 6.8 %collective-permute-start.11 = (bf16[96,512]{1,0:T(8,128)(2,1)S(1)}, bf16[96,512]{1,0:T(8,128)(2,1)S(1)}, u32[]{:S(2)}, u32[]{:S(2)}) collective-permute-start(bf16[96,512]{1,0:T(8,128)(2,1)S(1)} %get-tuple-element.46), channel_id=1, source_target_pairs={{0,1},{1,2},{2,3},{3,4},{4,5},{5,6},{6,7},{7,8},{8,9},{9,10},{10,1... | collective-permute-start | bytes 294920 | tf_op jit(solution)/shard_map/ppermute | solution.py:371
  86.8 20.4 %collective-permute-start.9 = (bf16[288,512]{1,0:T(8,128)(2,1)S(1)}, bf16[288,512]{1,0:T(8,128)(2,1)S(1)}, u32[]{:S(2)}, u32[]{:S(2)}) collective-permute-start(bf16[288,512]{1,0:T(8,128)(2,1)S(1)} %get-tuple-element.47), channel_id=1, source_target_pairs={{0,16},{1,17},{2,18},{3,19},{4,20},{5,21},{6,22},{7,23},{8,24},{9,... | collective-permute-start | bytes 884744 | tf_op jit(solution)/shard_map/ppermute | solution.py:371
  93.2 14.0 %collective-permute-start.10 = (bf16[96,512]{1,0:T(8,128)(2,1)S(1)}, bf16[96,512]{1,0:T(8,128)(2,1)S(1)}, u32[]{:S(2)}, u32[]{:S(2)}) collective-permute-start(bf16[96,512]{1,0:T(8,128)(2,1)S(1)} %get-tuple-element.45), channel_id=1, source_target_pairs={{0,17},{1,18},{2,19},{3,20},{4,21},{5,22},{6,23},{7,24},{8,25},{9,... | collective-permute-start | bytes 294920 | tf_op jit(solution)/shard_map/ppermute | solution.py:371
  93.6 9.2 %collective-permute-start.29 = (bf16[8,144,144]{2,1,0:T(8,128)(2,1)S(1)}, bf16[8,144,144]{2,1,0:T(8,128)(2,1)S(1)}, u32[]{:S(2)}, u32[]{:S(2)}) collective-permute-start(bf16[8,144,144]{2,1,0:T(8,128)(2,1)S(1)} %get-tuple-element.33), channel_id=1, source_target_pairs={{0,1},{1,0},{2,3},{3,2},{4,5},{5,4},{6,7},{7,6},{16,17},{17,16},{1... | collective-permute-start | bytes 995336 | tf_op jit(solution)/shard_map/ppermute | solution.py:343
  101.2 39.3 %collective-permute-start.19 = (bf16[2304,512]{1,0:T(8,128)(2,1)}, bf16[2304,512]{1,0:T(8,128)(2,1)}, u32[]{:S(2)}, u32[]{:S(2)}) collective-permute-start(bf16[2304,512]{1,0:T(8,128)(2,1)} %get-tuple-element.31), channel_id=1, source_target_pairs={{0,1},{1,0},{2,3},{3,2},{4,5},{5,4},{6,7},{7,6},{16,17},{17,16},{1... | collective-permute-start | bytes 7077896 | tf_op jit(solution)/shard_map/ppermute | solution.py:343
  101.3 34.1 %collective-permute-start.12 = (bf16[256,1536]{1,0:T(8,128)(2,1)S(1)}, bf16[256,1536]{1,0:T(8,128)(2,1)S(1)}, u32[]{:S(2)}, u32[]{:S(2)}) collective-permute-start(bf16[256,1536]{1,0:T(8,128)(2,1)S(1)} %get-tuple-element.29), channel_id=1, source_target_pairs={{0,1},{1,0},{2,3},{3,2},{4,5},{5,4},{6,7},{7,6},{16,17},{17,16},{1... | collective-permute-start | bytes 2359304 | tf_op jit(solution)/shard_map/ppermute | solution.py:343
  102.9 5.1 %collective-permute-start.32 = (bf16[2,144,144]{2,1,0:T(8,128)(2,1)S(1)}, bf16[2,144,144]{2,1,0:T(8,128)(2,1)S(1)}, u32[]{:S(2)}, u32[]{:S(2)}) collective-permute-start(bf16[2,144,144]{2,1,0:T(8,128)(2,1)S(1)} %get-tuple-element.43), channel_id=1, source_target_pairs={{0,6},{1,7},{2,0},{3,1},{4,2},{5,3},{6,4},{7,5},{16,22},{17,23},{1... | collective-permute-start | bytes 248840 | tf_op jit(solution)/shard_map/ppermute | solution.py:343
  107.2 5.6 %collective-permute-start.31 = (bf16[2,144,144]{2,1,0:T(8,128)(2,1)S(1)}, bf16[2,144,144]{2,1,0:T(8,128)(2,1)S(1)}, u32[]{:S(2)}, u32[]{:S(2)}) collective-permute-start(bf16[2,144,144]{2,1,0:T(8,128)(2,1)S(1)} %get-tuple-element.44), channel_id=1, source_target_pairs={{0,4},{1,5},{2,6},{3,7},{4,0},{5,1},{6,2},{7,3},{16,20},{17,21},{1... | collective-permute-start | bytes 248840 | tf_op jit(solution)/shard_map/ppermute | solution.py:343
  107.2 8.2 %collective-permute-start.30 = (bf16[2,144,144]{2,1,0:T(8,128)(2,1)S(1)}, bf16[2,144,144]{2,1,0:T(8,128)(2,1)S(1)}, u32[]{:S(2)}, u32[]{:S(2)}) collective-permute-start(bf16[2,144,144]{2,1,0:T(8,128)(2,1)S(1)} %get-tuple-element.42), channel_id=1, source_target_pairs={{0,2},{1,3},{2,4},{3,5},{4,6},{5,7},{6,0},{7,1},{16,18},{17,19},{1... | collective-permute-start | bytes 248840 | tf_op jit(solution)/shard_map/ppermute | solution.py:343
  115.5 6.1 %collective-permute-start.33 = (bf16[2,144,144]{2,1,0:T(8,128)(2,1)S(1)}, bf16[2,144,144]{2,1,0:T(8,128)(2,1)S(1)}, u32[]{:S(2)}, u32[]{:S(2)}) collective-permute-start(bf16[2,144,144]{2,1,0:T(8,128)(2,1)S(1)} %add_convert_fusion.11), channel_id=1, source_target_pairs={{0,8},{1,9},{2,10},{3,11},{4,12},{5,13},{6,14},{7,15},{16,24},{17,... | collective-permute-start | bytes 248840 | tf_op jit(solution)/shard_map/ppermute | solution.py:343
  121.7 4.6 %collective-permute-start.34 = (bf16[2,144,144]{2,1,0:T(8,128)(2,1)S(1)}, bf16[2,144,144]{2,1,0:T(8,128)(2,1)S(1)}, u32[]{:S(2)}, u32[]{:S(2)}) collective-permute-start(bf16[2,144,144]{2,1,0:T(8,128)(2,1)S(1)} %get-tuple-element.35), channel_id=1, source_target_pairs={{0,6},{1,7},{2,0},{3,1},{4,2},{5,3},{6,4},{7,5},{16,22},{17,23},{1... | collective-permute-start | bytes 248840 | tf_op jit(solution)/shard_map/ppermute | solution.py:343
  122.6 5.5 %collective-permute-start.35 = (bf16[2,144,144]{2,1,0:T(8,128)(2,1)S(1)}, bf16[2,144,144]{2,1,0:T(8,128)(2,1)S(1)}, u32[]{:S(2)}, u32[]{:S(2)}) collective-permute-start(bf16[2,144,144]{2,1,0:T(8,128)(2,1)S(1)} %get-tuple-element.35), channel_id=1, source_target_pairs={{0,4},{1,5},{2,6},{3,7},{4,0},{5,1},{6,2},{7,3},{16,20},{17,21},{1... | collective-permute-start | bytes 248840 | tf_op jit(solution)/shard_map/ppermute | solution.py:343
  125.4 7.4 %collective-permute-start.36 = (bf16[2,144,144]{2,1,0:T(8,128)(2,1)S(1)}, bf16[2,144,144]{2,1,0:T(8,128)(2,1)S(1)}, u32[]{:S(2)}, u32[]{:S(2)}) collective-permute-start(bf16[2,144,144]{2,1,0:T(8,128)(2,1)S(1)} %get-tuple-element.35), channel_id=1, source_target_pairs={{0,2},{1,3},{2,4},{3,5},{4,6},{5,7},{6,0},{7,1},{16,18},{17,19},{1... | collective-permute-start | bytes 248840 | tf_op jit(solution)/shard_map/ppermute | solution.py:343
  133.7 5.0 %collective-permute-start.37 = (bf16[1,8,144,144]{3,2,1,0:T(8,128)(2,1)S(1)}, bf16[1,8,144,144]{3,2,1,0:T(8,128)(2,1)}, u32[]{:S(2)}, u32[]{:S(2)}) collective-permute-start(bf16[1,8,144,144]{3,2,1,0:T(8,128)(2,1)S(1)} %bitcast.57), channel_id=1, source_target_pairs={{0,1},{1,0},{2,3},{3,2},{4,5},{5,4},{6,7},{7,6},{16,17},{17,16},{1... | collective-permute-start | bytes 995336 | tf_op jit(solution)/shard_map/ppermute | solution.py:343
  136.3 9.5 %collective-permute-start.15 = (bf16[64,1536]{1,0:T(8,128)(2,1)}, bf16[64,1536]{1,0:T(8,128)(2,1)S(1)}, u32[]{:S(2)}, u32[]{:S(2)}) collective-permute-start(bf16[64,1536]{1,0:T(8,128)(2,1)} %get-tuple-element.40), channel_id=1, source_target_pairs={{0,6},{1,7},{2,0},{3,1},{4,2},{5,3},{6,4},{7,5},{16,22},{17,23},{1... | collective-permute-start | bytes 589832 | tf_op jit(solution)/shard_map/ppermute | solution.py:343
  136.3 10.2 %collective-permute-start.14 = (bf16[64,1536]{1,0:T(8,128)(2,1)}, bf16[64,1536]{1,0:T(8,128)(2,1)}, u32[]{:S(2)}, u32[]{:S(2)}) collective-permute-start(bf16[64,1536]{1,0:T(8,128)(2,1)} %get-tuple-element.41), channel_id=1, source_target_pairs={{0,4},{1,5},{2,6},{3,7},{4,0},{5,1},{6,2},{7,3},{16,20},{17,21},{1... | collective-permute-start | bytes 589832 | tf_op jit(solution)/shard_map/ppermute | solution.py:343
  138.5 10.7 %collective-permute-start.13 = (bf16[64,1536]{1,0:T(8,128)(2,1)S(1)}, bf16[64,1536]{1,0:T(8,128)(2,1)}, u32[]{:S(2)}, u32[]{:S(2)}) collective-permute-start(bf16[64,1536]{1,0:T(8,128)(2,1)S(1)} %get-tuple-element.39), channel_id=1, source_target_pairs={{0,2},{1,3},{2,4},{3,5},{4,6},{5,7},{6,0},{7,1},{16,18},{17,19},{1... | collective-permute-start | bytes 589832 | tf_op jit(solution)/shard_map/ppermute | solution.py:343
  143.0 16.9 %collective-permute-start.22 = (bf16[576,512]{1,0:T(8,128)(2,1)S(1)}, bf16[576,512]{1,0:T(8,128)(2,1)S(1)}, u32[]{:S(2)}, u32[]{:S(2)}) collective-permute-start(bf16[576,512]{1,0:T(8,128)(2,1)S(1)} %get-tuple-element.37), channel_id=1, source_target_pairs={{0,6},{1,7},{2,0},{3,1},{4,2},{5,3},{6,4},{7,5},{16,22},{17,23},{1... | collective-permute-start | bytes 1769480 | tf_op jit(solution)/shard_map/ppermute | solution.py:343
  145.5 15.3 %collective-permute-start.21 = (bf16[576,512]{1,0:T(8,128)(2,1)S(1)}, bf16[576,512]{1,0:T(8,128)(2,1)S(1)}, u32[]{:S(2)}, u32[]{:S(2)}) collective-permute-start(bf16[576,512]{1,0:T(8,128)(2,1)S(1)} %get-tuple-element.38), channel_id=1, source_target_pairs={{0,4},{1,5},{2,6},{3,7},{4,0},{5,1},{6,2},{7,3},{16,20},{17,21},{1... | collective-permute-start | bytes 1769480 | tf_op jit(solution)/shard_map/ppermute | solution.py:343
  145.8 29.1 %collective-permute-start.20 = (bf16[576,512]{1,0:T(8,128)(2,1)S(1)}, bf16[576,512]{1,0:T(8,128)(2,1)S(1)}, u32[]{:S(2)}, u32[]{:S(2)}) collective-permute-start(bf16[576,512]{1,0:T(8,128)(2,1)S(1)} %get-tuple-element.36), channel_id=1, source_target_pairs={{0,2},{1,3},{2,4},{3,5},{4,6},{5,7},{6,0},{7,1},{16,18},{17,19},{1... | collective-permute-start | bytes 1769480 | tf_op jit(solution)/shard_map/ppermute | solution.py:343
  150.3 27.5 %collective-permute-start.18 = (bf16[16,1536]{1,0:T(8,128)(2,1)S(1)}, bf16[16,1536]{1,0:T(8,128)(2,1)S(1)}, u32[]{:S(2)}, u32[]{:S(2)}) collective-permute-start(bf16[16,1536]{1,0:T(8,128)(2,1)S(1)} %get-tuple-element.64), channel_id=1, source_target_pairs={{0,24},{1,25},{2,26},{3,27},{4,28},{5,29},{6,30},{7,31},{16,0},{17... | collective-permute-start | bytes 147464 | tf_op jit(solution)/shard_map/ppermute | solution.py:343
  150.4 27.7 %collective-permute-start.17 = (bf16[16,1536]{1,0:T(8,128)(2,1)S(1)}, bf16[16,1536]{1,0:T(8,128)(2,1)S(1)}, u32[]{:S(2)}, u32[]{:S(2)}) collective-permute-start(bf16[16,1536]{1,0:T(8,128)(2,1)S(1)} %get-tuple-element.65), channel_id=1, source_target_pairs={{0,8},{1,9},{2,10},{3,11},{4,12},{5,13},{6,14},{7,15},{16,24},{17,... | collective-permute-start | bytes 147464 | tf_op jit(solution)/shard_map/ppermute | solution.py:343
  159.9 18.2 %collective-permute-start.16 = (bf16[16,1536]{1,0:T(8,128)(2,1)S(1)}, bf16[16,1536]{1,0:T(8,128)(2,1)S(1)}, u32[]{:S(2)}, u32[]{:S(2)}) collective-permute-start(bf16[16,1536]{1,0:T(8,128)(2,1)S(1)} %get-tuple-element.63), channel_id=1, source_target_pairs={{0,16},{1,17},{2,18},{3,19},{4,20},{5,21},{6,22},{7,23},{16,8},{17... | collective-permute-start | bytes 147464 | tf_op jit(solution)/shard_map/ppermute | solution.py:343
  176.5 5.0 %collective-permute-start.25 = (bf16[144,512]{1,0:T(8,128)(2,1)S(1)}, bf16[144,512]{1,0:T(8,128)(2,1)S(1)}, u32[]{:S(2)}, u32[]{:S(2)}) collective-permute-start(bf16[144,512]{1,0:T(8,128)(2,1)S(1)} %get-tuple-element.54), channel_id=1, source_target_pairs={{0,24},{1,25},{2,26},{3,27},{4,28},{5,29},{6,30},{7,31},{16,0},{17... | collective-permute-start | bytes 442376 | tf_op jit(solution)/shard_map/ppermute | solution.py:343
  176.6 6.5 %collective-permute-start.24 = (bf16[144,512]{1,0:T(8,128)(2,1)S(1)}, bf16[144,512]{1,0:T(8,128)(2,1)S(1)}, u32[]{:S(2)}, u32[]{:S(2)}) collective-permute-start(bf16[144,512]{1,0:T(8,128)(2,1)S(1)} %get-tuple-element.55), channel_id=1, source_target_pairs={{0,8},{1,9},{2,10},{3,11},{4,12},{5,13},{6,14},{7,15},{16,24},{17,... | collective-permute-start | bytes 442376 | tf_op jit(solution)/shard_map/ppermute | solution.py:343
  177.8 9.2 %collective-permute-start.23 = (bf16[144,512]{1,0:T(8,128)(2,1)S(1)}, bf16[144,512]{1,0:T(8,128)(2,1)S(1)}, u32[]{:S(2)}, u32[]{:S(2)}) collective-permute-start(bf16[144,512]{1,0:T(8,128)(2,1)S(1)} %get-tuple-element.53), channel_id=1, source_target_pairs={{0,16},{1,17},{2,18},{3,19},{4,20},{5,21},{6,22},{7,23},{16,8},{17... | collective-permute-start | bytes 442376 | tf_op jit(solution)/shard_map/ppermute | solution.py:343
  187.2 3.0 %collective-permute-start.28 = (bf16[48,512]{1,0:T(8,128)(2,1)S(1)}, bf16[48,512]{1,0:T(8,128)(2,1)S(1)}, u32[]{:S(2)}, u32[]{:S(2)}) collective-permute-start(bf16[48,512]{1,0:T(8,128)(2,1)S(1)} %get-tuple-element.62), channel_id=1, source_target_pairs={{0,96},{1,97},{2,98},{3,99},{4,100},{5,101},{6,102},{7,103},{16,11... | collective-permute-start | bytes 147464 | tf_op jit(solution)/shard_map/ppermute | solution.py:343
  187.3 4.5 %collective-permute-start.27 = (bf16[48,512]{1,0:T(8,128)(2,1)S(1)}, bf16[48,512]{1,0:T(8,128)(2,1)S(1)}, u32[]{:S(2)}, u32[]{:S(2)}) collective-permute-start(bf16[48,512]{1,0:T(8,128)(2,1)S(1)} %get-tuple-element.61), channel_id=1, source_target_pairs={{0,64},{1,65},{2,66},{3,67},{4,68},{5,69},{6,70},{7,71},{16,80},{1... | collective-permute-start | bytes 147464 | tf_op jit(solution)/shard_map/ppermute | solution.py:343
  188.5 4.8 %collective-permute-start.26 = (bf16[48,512]{1,0:T(8,128)(2,1)S(1)}, bf16[48,512]{1,0:T(8,128)(2,1)S(1)}, u32[]{:S(2)}, u32[]{:S(2)}) collective-permute-start(bf16[48,512]{1,0:T(8,128)(2,1)S(1)} %get-tuple-element.60), channel_id=1, source_target_pairs={{0,32},{1,33},{2,34},{3,35},{4,36},{5,37},{6,38},{7,39},{16,48},{1... | collective-permute-start | bytes 147464 | tf_op jit(solution)/shard_map/ppermute | solution.py:343
